TPU v7x, 512 devices: a whole 4x4x16 slice. The times are simulated.
512 devices in a mesh: stream: 16 (over z_lo, y), cross: 32 (over z_hi, x, core).
Axes of the slice: x: 4, y: 4, z: 16 (z_hi: 4, z_lo: 4; z = z_hi * 4 + z_lo), core: 2. Of those that a mesh axis runs over, the one named last changes fastest.
Arguments:
- vof: bfloat16 [6144, 512], P(('stream', 'cross')), may hold values from 0 to 1
- target: bfloat16 [6144, 512], P(('stream', 'cross')), may hold values from -21 to 21
- neighbours: int32 [6144, 26], P(('stream', 'cross')), may hold values from -1 to 6143, as said below
- live_blocks: int32 [512], P(('stream', 'cross')), may hold values from 2 to 12, as said below
- pick: int32 [512, 2], P(('stream', 'cross')), may hold values from -1 to 191, as said below
- w_first: bfloat16 [125, 128], replicated, may hold values from -0.5 to 0.5
- w_mid: bfloat16 [2, 128, 128], replicated, may hold values from -0.5 to 0.5
- w_last: bfloat16 [128], replicated, may hold values from -0.5 to 0.5
Outputs:
- prediction: float32 [4096, 512], P(('stream', 'cross'))
- grad_first: float32 [125, 128], replicated
- grad_mid: float32 [2, 128, 128], replicated
- grad_last: float32 [128], replicated
Inputs may be any that keep to these rules, and one draw needn't show every extreme that they name: Home slots 0 to live_blocks[d] - 1 of device d hold interface blocks and the rest are empty; in every slab 8 devices hold more than 6 blocks and the others at most 6. `neighbours`: an entry names a live home slot of a device whose stream index and cross index each differ from those of the block's own device by at most one. `pick`: in each slab every live home slot 6 + j of the device with cross index c is named, as c * 6 + j, by exactly one entry of one device of that slab; devices holding more than 6 blocks name none.
All inputs are finite; a program needn't handle non-finite values.
Results may differ from a plain program's by a relative error of at most 0.003.
The roundings to bfloat16 on the way count: a program that leaves them out, or rounds other values in their place, can miss the bound.
Values may be sent and summed in bfloat16 or wider, within the bound.
A program may use at most 128 MiB of HBM per device.

v0:
```python
import jax
import jax.numpy as jnp
from jax import lax
from jax.sharding import PartitionSpec as P

FEAT = 125
BE = 8
KEEP = 6
RECV = 2
PADROW = 1792


def from_behind(block, axis, distance):
    devices = range(lax.axis_size(axis))
    route = [(i - distance, i) for i in devices if i - distance in devices]
    return lax.ppermute(block, axis, route)


def assemble(center, border, block_edge):
    number = center.shape[0]
    pieces = jnp.concatenate([border[:, :13], center[:, None], border[:, 13:]], axis=1)
    shaped = pieces.reshape(number, 3, 3, 3, block_edge, block_edge, block_edge)
    shaped = shaped.transpose(0, 1, 4, 2, 5, 3, 6).reshape(
        number, 3 * block_edge, 3 * block_edge, 3 * block_edge
    )
    lower = block_edge - 2
    upper = 2 * block_edge + 2
    return shaped[:, lower:upper, lower:upper, lower:upper]


def stencil(padded, block_edge):
    columns = []
    for along_x in range(5):
        for along_y in range(5):
            for along_z in range(5):
                window = padded[
                    :,
                    along_x : along_x + block_edge,
                    along_y : along_y + block_edge,
                    along_z : along_z + block_edge,
                ]
                columns.append(window.reshape(-1))
    return jnp.stack(columns)


def contract_rows(former, latter):
    return lax.dot_general(
        former, latter, (((0,), (0,)), ((), ())), preferred_element_type=jnp.float32
    )


def contract_cols(former, latter):
    return lax.dot_general(
        former, latter, (((1,), (1,)), ((), ())), preferred_element_type=jnp.float32
    )


def train_terms(features, target_row, weight_mask, w_first, w_mid, w_last, loss_scale):
    hidden_one = jnp.tanh(contract_rows(w_first, features)).astype(jnp.bfloat16)
    hidden_two = jnp.tanh(contract_rows(w_mid[0], hidden_one)).astype(jnp.bfloat16)
    hidden_three = jnp.tanh(contract_rows(w_mid[1], hidden_two)).astype(jnp.bfloat16)
    predicted = jnp.dot(w_last, hidden_three, preferred_element_type=jnp.float32) * weight_mask
    residual = ((predicted - target_row.astype(jnp.float32)) * weight_mask / loss_scale).astype(
        jnp.bfloat16
    )
    grad_last = jnp.dot(hidden_three, residual, preferred_element_type=jnp.float32)
    slope_three = 1.0 - jnp.square(hidden_three.astype(jnp.float32))
    delta_three = (
        w_last.astype(jnp.float32)[:, None] * residual.astype(jnp.float32)[None, :] * slope_three
    ).astype(jnp.bfloat16)
    grad_third = contract_cols(hidden_two, delta_three)
    slope_two = 1.0 - jnp.square(hidden_two.astype(jnp.float32))
    delta_two = (
        jnp.dot(w_mid[1], delta_three, preferred_element_type=jnp.float32) * slope_two
    ).astype(jnp.bfloat16)
    grad_second = contract_cols(hidden_one, delta_two)
    slope_one = 1.0 - jnp.square(hidden_one.astype(jnp.float32))
    delta_one = (
        jnp.dot(w_mid[0], delta_two, preferred_element_type=jnp.float32) * slope_one
    ).astype(jnp.bfloat16)
    grad_first = contract_cols(features, delta_one)
    return (predicted, grad_first, jnp.stack([grad_second, grad_third]), grad_last)


def shards(vof, target, neighbours, live_blocks, pick, w_first, w_mid, w_last):
    home_blocks = vof.shape[0]
    cell_count = vof.shape[1]
    cross_size = lax.axis_size("cross")
    stream_size = lax.axis_size("stream")
    slab_index = lax.axis_index("stream")
    cross_index = lax.axis_index("cross")
    below = from_behind(vof, "stream", 1)
    above = from_behind(vof, "stream", -1)
    column = jnp.stack([below, vof, above])
    left = from_behind(column, "cross", 1)
    right = from_behind(column, "cross", -1)
    beside_all = jnp.stack([left, column, right], axis=1)
    table = jnp.concatenate(
        [beside_all.reshape(9 * home_blocks, cell_count), jnp.zeros((1, cell_count), vof.dtype)],
        axis=0,
    )
    owner_device = neighbours // home_blocks
    slab_step = owner_device // cross_size - slab_index + 1
    cross_step = owner_device % cross_size - cross_index + 1
    lookup = (slab_step * 3 + cross_step) * home_blocks + neighbours % home_blocks
    lookup = jnp.where(neighbours < 0, 9 * home_blocks, lookup)
    border = jnp.take(table, lookup, axis=0)
    padded = assemble(vof, border, BE)
    live_count = live_blocks[0]
    home_mask = (jnp.arange(home_blocks) < live_count).astype(jnp.float32)
    loss_scale = float(cell_count * KEEP * cross_size * stream_size)
    chosen = pick[0]
    padded_edge = padded.shape[1]
    flat_rows = padded.reshape(home_blocks, padded_edge**3)
    flat_rows = jnp.pad(flat_rows, ((0, 0), (0, PADROW - padded_edge**3)))
    pieces = (
        lax.all_gather(flat_rows[KEEP:], "cross", axis=0, tiled=True),
        lax.all_gather(target[KEEP:], "cross", axis=0, tiled=True),
    )
    selector = (chosen[:, None] == jnp.arange(pieces[0].shape[0])[None, :]).astype(jnp.bfloat16)
    got_blocks = jnp.dot(selector, pieces[0], preferred_element_type=jnp.float32)
    got_targets = jnp.dot(selector, pieces[1], preferred_element_type=jnp.float32)
    got_blocks = got_blocks.astype(jnp.bfloat16)
    got_targets = got_targets.astype(jnp.bfloat16)
    got_blocks = got_blocks[:, : padded_edge**3].reshape(
        RECV, padded_edge, padded_edge, padded_edge
    )
    work_padded = jnp.concatenate([padded[:KEEP], got_blocks], axis=0)
    work_target = jnp.concatenate([target[:KEEP], got_targets], axis=0)
    block_mask = jnp.concatenate([home_mask[:KEEP], (chosen >= 0).astype(jnp.float32)])
    predicted, grad_first, grad_mid, grad_last = train_terms(
        stencil(work_padded, BE),
        work_target.reshape(-1),
        jnp.repeat(block_mask, cell_count),
        w_first,
        w_mid,
        w_last,
        loss_scale,
    )
    prediction = predicted.reshape(KEEP + RECV, cell_count)
    hidden_size = grad_last.shape[0]
    packed = jnp.concatenate(
        [
            grad_first,
            grad_last[None, :],
            jnp.zeros((128 - FEAT - 1, hidden_size), jnp.float32),
            grad_mid.reshape(2 * hidden_size, hidden_size),
        ],
        axis=0,
    )
    summed = lax.psum(packed, ("stream", "cross"))
    return (
        prediction,
        summed[:FEAT],
        summed[128:].reshape(2, hidden_size, hidden_size),
        summed[FEAT],
    )


def solution(mesh):
    return jax.shard_map(
        shards,
        mesh=mesh,
        in_specs=(
            P(("stream", "cross"), None),
            P(("stream", "cross"), None),
            P(("stream", "cross"), None),
            P(("stream", "cross")),
            P(("stream", "cross"), None),
            P(),
            P(),
            P(),
        ),
        out_specs=(P(("stream", "cross"), None), P(), P(), P()),
        check_vma=False,
    )
```

profile of v0, /device:TPU:1, one launch (start us, length us, event | category | flops | bytes accessed | tf_op | source)
XLA Modules:
  0.0 796.8 jit_solution(742776914680141394)
XLA Ops:
  7.2 4.0 collective-permute-start
  11.3 1.3 collective-permute-start.1
  12.6 0.8 fusion.44
  13.4 60.5 %all-gather.1 = bf16[32,6,512]{2,1,0:T(8,128)(2,1)S(1)} all-gather(bf16[1,6,512]{2,1,0:T(8,128)(2,1)S(1)} %get-tuple-element.139), channel_id=1, replica_groups=mesh['stream'=16,'cross'=32] {'cross'}, dimensions={0}, use_global_device_ids=true | all-gather | bytes 202752 | tf_op jit(solution)/shard_map/all_gather | solution.py:118
  75.4 0.8 convolution_convert_fusion
  77.8 1.9 collective-permute-start.2
  79.7 2.4 collective-permute-start.3
  84.1 1.2 convert_element_type.65
  86.1 2.0 gather_fusion
  88.6 7.5 reshape.47
  96.0 12.7 %copy.151 = bf16[12,3,8,3,8,3,8]{0,6,5,4,3,2,1:T(8,128)(2,1)} copy(bf16[12,3,8,3,8,3,8]{6,4,2,5,3,1,0:T(8,128)(2,1)} %bitcast.318) | data formatting | bytes 663552 | tf_op jit(solution)/shard_map/transpose | solution.py:23
  108.7 1.4 slice.565
  110.2 1.4 slice.564
  112.1 53.0 %all-gather = bf16[32,6,1792]{2,1,0:T(8,128)(2,1)S(1)} all-gather(bf16[1,6,1792]{2,1,0:T(8,128)(2,1)S(1)} %fusion.18), channel_id=1, replica_groups=mesh['stream'=16,'cross'=32] {'cross'}, dimensions={0}, use_global_device_ids=true | all-gather | bytes 709632 | tf_op jit(solution)/shard_map/all_gather | solution.py:117
  165.8 1.0 copy.153
  167.3 1.2 slice_maximum_fusion.12
  168.4 1.2 slice_maximum_fusion.13
  169.6 1.2 slice_maximum_fusion.14
  170.8 1.3 slice_maximum_fusion.15
  172.1 1.2 slice_maximum_fusion.16
  173.4 1.1 slice_maximum_fusion.17
  174.5 1.2 slice_maximum_fusion.18
  175.7 1.3 slice_maximum_fusion.19
  176.9 1.3 slice_maximum_fusion.20
  178.2 1.3 slice_maximum_fusion.21
  179.4 1.3 slice_maximum_fusion.22
  180.7 1.1 slice_maximum_fusion.23
  181.8 1.3 slice_maximum_fusion.24
  183.1 1.3 slice_maximum_fusion.25
  184.4 1.3 slice_maximum_fusion.26
  185.6 1.3 slice_maximum_fusion.27
  186.9 1.2 slice_maximum_fusion.28
  188.0 1.2 slice_maximum_fusion.29
  189.2 1.2 slice_maximum_fusion.11
  190.4 1.3 slice_maximum_fusion.10
  191.6 1.2 slice_maximum_fusion.9
  192.9 1.1 slice_maximum_fusion.8
  194.0 1.4 slice_maximum_fusion.7
  195.4 1.2 slice_maximum_fusion.6
  196.6 1.3 slice_maximum_fusion.5
  197.9 1.2 slice_maximum_fusion.4
  199.1 1.1 slice_maximum_fusion.3
  209.2 1.2 copy.200
  212.5 0.8 stack_reshape.423
  216.8 0.8 stack_reshape.427
  235.2 0.8 stack_reshape.444
  241.6 0.8 stack_reshape.450
  252.2 0.8 stack_reshape.460
  253.3 0.8 stack_reshape.461
  266.5 0.8 stack_reshape.473
  269.7 0.8 stack_reshape.476
  277.2 0.8 stack_reshape.483
  281.1 1.2 copy.191
  293.2 0.8 stack_reshape.491
  310.7 9.6 %stack.44 = bf16[125,4096]{1,0:T(8,128)(2,1)S(1)} concatenate(bf16[1,4096]{1,0:T(2,128)(2,1)S(1)} %stack_reshape.375, bf16[1,4096]{1,0:T(2,128)(2,1)S(1)} %stack_reshape.376, bf16[1,4096]{1,0:T(2,128)(2,1)S(1)} %stack_reshape.377, bf16[1,4096]{1,0:T(2,128)(2,1)S(1)} %stack_reshape.378, bf16[1,4096]{1,0:T(2,128)(2,1)S(1)} %stack_reshape.379, bf16[1,4096]{1,0:T(2,128)(2,1)S(1)} %stack_reshape.380, ...), dimensions={0} | concatenate | bytes 2048000 | tf_op jit(solution)/shard_map/stack | solution.py:43
  322.2 1.8 fusion.3
  324.0 2.1 fusion.6
  326.1 1.8 convolution_bitcast_fusion.1
  327.9 1.1 convolution_bitcast_fusion
  329.3 0.8 pad_maximum_fusion.1
  330.7 454.9 %all-reduce.4.cloned.1.call-done = f32[384,128]{1,0:T(8,128)} async-done(((f32[384,128]{1,0:T(8,128)}), f32[384,128]{1,0:T(8,128)}) %all-reduce.4.cloned.1.call-update) | async-done | bytes 196624 | tf_op jit(solution)/shard_map/psum | solution.py:151
  785.5 1.6 slice.816
  787.1 1.5 slice.815
  788.6 1.2 slice_bitcast_fusion.1
  (594 shorter events, 107.9 us)
Async XLA Ops:
  7.2 313.1 %copy-start = (bf16[125,128]{1,0:T(8,128)(2,1)S(1)}, bf16[125,128]{1,0:T(8,128)(2,1)}, u32[]{:S(2)}) copy-start(bf16[125,128]{1,0:T(8,128)(2,1)} %param.13) | copy-start | bytes 96004
  7.2 778.4 %all-reduce.4.cloned.1.call-start = ((), (), s32[]{:S(2)}) async-start(), calls=%async_computation | async-start | bytes 393216 | tf_op jit(solution)/shard_map/psum | solution.py:151
  7.2 69.8 %collective-permute-start = (bf16[12,512]{1,0:T(8,128)(2,1)}, bf16[12,512]{1,0:T(8,128)(2,1)S(1)}, u32[]{:S(2)}, u32[]{:S(2)}) collective-permute-start(bf16[12,512]{1,0:T(8,128)(2,1)} %param.8), channel_id=1, source_target_pairs={{0,32},{32,64},{64,96},{96,128},{128,160},{160,192},{192,224},{224... | collective-permute-start | bytes 36872 | tf_op jit(solution)/shard_map/ppermute | solution.py:16
  11.3 65.8 %collective-permute-start.1 = (bf16[12,512]{1,0:T(8,128)(2,1)}, bf16[12,512]{1,0:T(8,128)(2,1)S(1)}, u32[]{:S(2)}, u32[]{:S(2)}) collective-permute-start(bf16[12,512]{1,0:T(8,128)(2,1)} %param.8), channel_id=1, source_target_pairs={{32,0},{64,32},{96,64},{128,96},{160,128},{192,160},{224,192},{256... | collective-permute-start | bytes 36872 | tf_op jit(solution)/shard_map/ppermute | solution.py:16
  77.8 8.2 %collective-permute-start.2 = (bf16[3,12,512]{2,1,0:T(8,128)(2,1)S(1)}, bf16[3,12,512]{2,1,0:T(8,128)(2,1)S(1)}, u32[]{:S(2)}, u32[]{:S(2)}) collective-permute-start(bf16[3,12,512]{2,1,0:T(8,128)(2,1)S(1)} %get-tuple-element.137), channel_id=1, source_target_pairs={{0,1},{1,2},{2,3},{3,4},{4,5},{5,6},{6,7},{7,8},{8,9},{9,10},{10,1... | collective-permute-start | bytes 110600 | tf_op jit(solution)/shard_map/ppermute | solution.py:16
  79.7 6.2 collective-permute-start.3
  111.6 53.7 %copy-start.151 = (s32[1,2]{1,0:T(1,128)S(1)}, s32[1,2]{1,0:T(1,128)}, u32[]{:S(2)}) copy-start(s32[1,2]{1,0:T(1,128)} %param.12) | copy-start | bytes 28
  204.8 11.7 %copy-start.97 = (bf16[8,8,8,8]{0,3,2,1:T(8,128)(2,1)S(1)}, bf16[8,8,8,8]{0,3,2,1:T(8,128)(2,1)}, u32[]{:S(2)}) copy-start(bf16[8,8,8,8]{0,3,2,1:T(8,128)(2,1)} %get-tuple-element.79) | copy-start | bytes 24580
  205.2 12.3 %copy-start.96 = (bf16[8,8,8,8]{0,3,2,1:T(8,128)(2,1)S(1)}, bf16[8,8,8,8]{0,3,2,1:T(8,128)(2,1)}, u32[]{:S(2)}) copy-start(bf16[8,8,8,8]{0,3,2,1:T(8,128)(2,1)} %get-tuple-element.80) | copy-start | bytes 24580
  206.3 12.3 %copy-start.95 = (bf16[8,8,8,8]{0,3,2,1:T(8,128)(2,1)S(1)}, bf16[8,8,8,8]{0,3,2,1:T(8,128)(2,1)}, u32[]{:S(2)}) copy-start(bf16[8,8,8,8]{0,3,2,1:T(8,128)(2,1)} %get-tuple-element.81) | copy-start | bytes 24580
  207.4 12.3 %copy-start.94 = (bf16[8,8,8,8]{0,3,2,1:T(8,128)(2,1)S(1)}, bf16[8,8,8,8]{0,3,2,1:T(8,128)(2,1)}, u32[]{:S(2)}) copy-start(bf16[8,8,8,8]{0,3,2,1:T(8,128)(2,1)} %get-tuple-element.83) | copy-start | bytes 24580
  208.4 12.3 %copy-start.93 = (bf16[8,8,8,8]{0,3,2,1:T(8,128)(2,1)S(1)}, bf16[8,8,8,8]{0,3,2,1:T(8,128)(2,1)}, u32[]{:S(2)}) copy-start(bf16[8,8,8,8]{0,3,2,1:T(8,128)(2,1)} %get-tuple-element.84) | copy-start | bytes 24580
  210.4 11.5 %copy-start.92 = (bf16[8,8,8,8]{0,3,2,1:T(8,128)(2,1)S(1)}, bf16[8,8,8,8]{0,3,2,1:T(8,128)(2,1)}, u32[]{:S(2)}) copy-start(bf16[8,8,8,8]{0,3,2,1:T(8,128)(2,1)} %get-tuple-element.85) | copy-start | bytes 24580
  211.5 11.5 %copy-start.91 = (bf16[8,8,8,8]{0,3,2,1:T(8,128)(2,1)S(1)}, bf16[8,8,8,8]{0,3,2,1:T(8,128)(2,1)}, u32[]{:S(2)}) copy-start(bf16[8,8,8,8]{0,3,2,1:T(8,128)(2,1)} %get-tuple-element.87) | copy-start | bytes 24580
  212.5 11.5 %copy-start.90 = (bf16[8,8,8,8]{0,3,2,1:T(8,128)(2,1)S(1)}, bf16[8,8,8,8]{0,3,2,1:T(8,128)(2,1)}, u32[]{:S(2)}) copy-start(bf16[8,8,8,8]{0,3,2,1:T(8,128)(2,1)} %get-tuple-element.88) | copy-start | bytes 24580
  213.6 11.7 %copy-start.89 = (bf16[8,8,8,8]{0,3,2,1:T(8,128)(2,1)S(1)}, bf16[8,8,8,8]{0,3,2,1:T(8,128)(2,1)}, u32[]{:S(2)}) copy-start(bf16[8,8,8,8]{0,3,2,1:T(8,128)(2,1)} %get-tuple-element.89) | copy-start | bytes 24580
  214.7 11.7 %copy-start.88 = (bf16[8,8,8,8]{0,3,2,1:T(8,128)(2,1)S(1)}, bf16[8,8,8,8]{0,3,2,1:T(8,128)(2,1)}, u32[]{:S(2)}) copy-start(bf16[8,8,8,8]{0,3,2,1:T(8,128)(2,1)} %get-tuple-element.91) | copy-start | bytes 24580
  215.7 11.7 %copy-start.87 = (bf16[8,8,8,8]{0,3,2,1:T(8,128)(2,1)S(1)}, bf16[8,8,8,8]{0,3,2,1:T(8,128)(2,1)}, u32[]{:S(2)}) copy-start(bf16[8,8,8,8]{0,3,2,1:T(8,128)(2,1)} %get-tuple-element.92) | copy-start | bytes 24580
  216.8 11.7 %copy-start.86 = (bf16[8,8,8,8]{0,3,2,1:T(8,128)(2,1)S(1)}, bf16[8,8,8,8]{0,3,2,1:T(8,128)(2,1)}, u32[]{:S(2)}) copy-start(bf16[8,8,8,8]{0,3,2,1:T(8,128)(2,1)} %get-tuple-element.93) | copy-start | bytes 24580
  217.9 11.7 %copy-start.85 = (bf16[8,8,8,8]{0,3,2,1:T(8,128)(2,1)S(1)}, bf16[8,8,8,8]{0,3,2,1:T(8,128)(2,1)}, u32[]{:S(2)}) copy-start(bf16[8,8,8,8]{0,3,2,1:T(8,128)(2,1)} %get-tuple-element.95) | copy-start | bytes 24580
  218.9 11.6 %copy-start.84 = (bf16[8,8,8,8]{0,3,2,1:T(8,128)(2,1)S(1)}, bf16[8,8,8,8]{0,3,2,1:T(8,128)(2,1)}, u32[]{:S(2)}) copy-start(bf16[8,8,8,8]{0,3,2,1:T(8,128)(2,1)} %get-tuple-element.96) | copy-start | bytes 24580
  220.0 11.6 %copy-start.83 = (bf16[8,8,8,8]{0,3,2,1:T(8,128)(2,1)S(1)}, bf16[8,8,8,8]{0,3,2,1:T(8,128)(2,1)}, u32[]{:S(2)}) copy-start(bf16[8,8,8,8]{0,3,2,1:T(8,128)(2,1)} %get-tuple-element.97) | copy-start | bytes 24580
  221.1 11.6 %copy-start.82 = (bf16[8,8,8,8]{0,3,2,1:T(8,128)(2,1)S(1)}, bf16[8,8,8,8]{0,3,2,1:T(8,128)(2,1)}, u32[]{:S(2)}) copy-start(bf16[8,8,8,8]{0,3,2,1:T(8,128)(2,1)} %get-tuple-element.99) | copy-start | bytes 24580
  222.1 11.7 %copy-start.81 = (bf16[8,8,8,8]{0,3,2,1:T(8,128)(2,1)S(1)}, bf16[8,8,8,8]{0,3,2,1:T(8,128)(2,1)}, u32[]{:S(2)}) copy-start(bf16[8,8,8,8]{0,3,2,1:T(8,128)(2,1)} %get-tuple-element.100) | copy-start | bytes 24580
  223.2 11.6 %copy-start.80 = (bf16[8,8,8,8]{0,3,2,1:T(8,128)(2,1)S(1)}, bf16[8,8,8,8]{0,3,2,1:T(8,128)(2,1)}, u32[]{:S(2)}) copy-start(bf16[8,8,8,8]{0,3,2,1:T(8,128)(2,1)} %get-tuple-element.101) | copy-start | bytes 24580
  224.5 11.4 %copy-start.79 = (bf16[8,8,8,8]{0,3,2,1:T(8,128)(2,1)S(1)}, bf16[8,8,8,8]{0,3,2,1:T(8,128)(2,1)}, u32[]{:S(2)}) copy-start(bf16[8,8,8,8]{0,3,2,1:T(8,128)(2,1)} %get-tuple-element.103) | copy-start | bytes 24580
  225.6 11.5 %copy-start.78 = (bf16[8,8,8,8]{0,3,2,1:T(8,128)(2,1)S(1)}, bf16[8,8,8,8]{0,3,2,1:T(8,128)(2,1)}, u32[]{:S(2)}) copy-start(bf16[8,8,8,8]{0,3,2,1:T(8,128)(2,1)} %get-tuple-element.104) | copy-start | bytes 24580
  226.6 11.4 %copy-start.77 = (bf16[8,8,8,8]{0,3,2,1:T(8,128)(2,1)S(1)}, bf16[8,8,8,8]{0,3,2,1:T(8,128)(2,1)}, u32[]{:S(2)}) copy-start(bf16[8,8,8,8]{0,3,2,1:T(8,128)(2,1)} %get-tuple-element.105) | copy-start | bytes 24580
  227.7 11.5 %copy-start.76 = (bf16[8,8,8,8]{0,3,2,1:T(8,128)(2,1)S(1)}, bf16[8,8,8,8]{0,3,2,1:T(8,128)(2,1)}, u32[]{:S(2)}) copy-start(bf16[8,8,8,8]{0,3,2,1:T(8,128)(2,1)} %get-tuple-element.107) | copy-start | bytes 24580
  228.8 11.5 %copy-start.75 = (bf16[8,8,8,8]{0,3,2,1:T(8,128)(2,1)S(1)}, bf16[8,8,8,8]{0,3,2,1:T(8,128)(2,1)}, u32[]{:S(2)}) copy-start(bf16[8,8,8,8]{0,3,2,1:T(8,128)(2,1)} %get-tuple-element.108) | copy-start | bytes 24580
  229.8 11.5 %copy-start.74 = (bf16[8,8,8,8]{0,3,2,1:T(8,128)(2,1)S(1)}, bf16[8,8,8,8]{0,3,2,1:T(8,128)(2,1)}, u32[]{:S(2)}) copy-start(bf16[8,8,8,8]{0,3,2,1:T(8,128)(2,1)} %get-tuple-element.109) | copy-start | bytes 24580
  230.9 11.5 %copy-start.73 = (bf16[8,8,8,8]{0,3,2,1:T(8,128)(2,1)S(1)}, bf16[8,8,8,8]{0,3,2,1:T(8,128)(2,1)}, u32[]{:S(2)}) copy-start(bf16[8,8,8,8]{0,3,2,1:T(8,128)(2,1)} %get-tuple-element.111) | copy-start | bytes 24580
  232.0 11.5 %copy-start.72 = (bf16[8,8,8,8]{0,3,2,1:T(8,128)(2,1)S(1)}, bf16[8,8,8,8]{0,3,2,1:T(8,128)(2,1)}, u32[]{:S(2)}) copy-start(bf16[8,8,8,8]{0,3,2,1:T(8,128)(2,1)} %get-tuple-element.112) | copy-start | bytes 24580
  233.0 11.4 %copy-start.71 = (bf16[8,8,8,8]{0,3,2,1:T(8,128)(2,1)S(1)}, bf16[8,8,8,8]{0,3,2,1:T(8,128)(2,1)}, u32[]{:S(2)}) copy-start(bf16[8,8,8,8]{0,3,2,1:T(8,128)(2,1)} %get-tuple-element.113) | copy-start | bytes 24580
  234.1 11.4 %copy-start.70 = (bf16[8,8,8,8]{0,3,2,1:T(8,128)(2,1)S(1)}, bf16[8,8,8,8]{0,3,2,1:T(8,128)(2,1)}, u32[]{:S(2)}) copy-start(bf16[8,8,8,8]{0,3,2,1:T(8,128)(2,1)} %get-tuple-element.115) | copy-start | bytes 24580
  235.2 11.4 %copy-start.69 = (bf16[8,8,8,8]{0,3,2,1:T(8,128)(2,1)S(1)}, bf16[8,8,8,8]{0,3,2,1:T(8,128)(2,1)}, u32[]{:S(2)}) copy-start(bf16[8,8,8,8]{0,3,2,1:T(8,128)(2,1)} %get-tuple-element.116) | copy-start | bytes 24580
  241.6 11.4 %copy-start.63 = (bf16[8,8,8,8]{0,3,2,1:T(8,128)(2,1)S(1)}, bf16[8,8,8,8]{0,3,2,1:T(8,128)(2,1)}, u32[]{:S(2)}) copy-start(bf16[8,8,8,8]{0,3,2,1:T(8,128)(2,1)} %get-tuple-element.124) | copy-start | bytes 24580
  242.6 11.4 %copy-start.62 = (bf16[8,8,8,8]{0,3,2,1:T(8,128)(2,1)S(1)}, bf16[8,8,8,8]{0,3,2,1:T(8,128)(2,1)}, u32[]{:S(2)}) copy-start(bf16[8,8,8,8]{0,3,2,1:T(8,128)(2,1)} %get-tuple-element.125) | copy-start | bytes 24580
  243.7 11.5 %copy-start.61 = (bf16[8,8,8,8]{0,3,2,1:T(8,128)(2,1)S(1)}, bf16[8,8,8,8]{0,3,2,1:T(8,128)(2,1)}, u32[]{:S(2)}) copy-start(bf16[8,8,8,8]{0,3,2,1:T(8,128)(2,1)} %get-tuple-element.127) | copy-start | bytes 24580
  244.8 11.5 %copy-start.60 = (bf16[8,8,8,8]{0,3,2,1:T(8,128)(2,1)S(1)}, bf16[8,8,8,8]{0,3,2,1:T(8,128)(2,1)}, u32[]{:S(2)}) copy-start(bf16[8,8,8,8]{0,3,2,1:T(8,128)(2,1)} %get-tuple-element.128) | copy-start | bytes 24580
  245.8 11.5 %copy-start.59 = (bf16[8,8,8,8]{0,3,2,1:T(8,128)(2,1)S(1)}, bf16[8,8,8,8]{0,3,2,1:T(8,128)(2,1)}, u32[]{:S(2)}) copy-start(bf16[8,8,8,8]{0,3,2,1:T(8,128)(2,1)} %get-tuple-element.129) | copy-start | bytes 24580
  246.9 11.5 %copy-start.58 = (bf16[8,8,8,8]{0,3,2,1:T(8,128)(2,1)S(1)}, bf16[8,8,8,8]{0,3,2,1:T(8,128)(2,1)}, u32[]{:S(2)}) copy-start(bf16[8,8,8,8]{0,3,2,1:T(8,128)(2,1)} %get-tuple-element.131) | copy-start | bytes 24580
  248.0 11.5 %copy-start.57 = (bf16[8,8,8,8]{0,3,2,1:T(8,128)(2,1)S(1)}, bf16[8,8,8,8]{0,3,2,1:T(8,128)(2,1)}, u32[]{:S(2)}) copy-start(bf16[8,8,8,8]{0,3,2,1:T(8,128)(2,1)} %get-tuple-element.132) | copy-start | bytes 24580
  249.0 11.4 %copy-start.56 = (bf16[8,8,8,8]{0,3,2,1:T(8,128)(2,1)S(1)}, bf16[8,8,8,8]{0,3,2,1:T(8,128)(2,1)}, u32[]{:S(2)}) copy-start(bf16[8,8,8,8]{0,3,2,1:T(8,128)(2,1)} %get-tuple-element.133) | copy-start | bytes 24580
  250.1 11.8 %copy-start.55 = (bf16[8,8,8,8]{0,3,2,1:T(8,128)(2,1)S(1)}, bf16[8,8,8,8]{0,3,2,1:T(8,128)(2,1)}, u32[]{:S(2)}) copy-start(bf16[8,8,8,8]{0,3,2,1:T(8,128)(2,1)} %get-tuple-element.130) | copy-start | bytes 24580
  251.2 11.8 %copy-start.54 = (bf16[8,8,8,8]{0,3,2,1:T(8,128)(2,1)S(1)}, bf16[8,8,8,8]{0,3,2,1:T(8,128)(2,1)}, u32[]{:S(2)}) copy-start(bf16[8,8,8,8]{0,3,2,1:T(8,128)(2,1)} %get-tuple-element.126) | copy-start | bytes 24580
  252.2 11.8 %copy-start.53 = (bf16[8,8,8,8]{0,3,2,1:T(8,128)(2,1)S(1)}, bf16[8,8,8,8]{0,3,2,1:T(8,128)(2,1)}, u32[]{:S(2)}) copy-start(bf16[8,8,8,8]{0,3,2,1:T(8,128)(2,1)} %get-tuple-element.122) | copy-start | bytes 24580
  253.3 11.8 %copy-start.52 = (bf16[8,8,8,8]{0,3,2,1:T(8,128)(2,1)S(1)}, bf16[8,8,8,8]{0,3,2,1:T(8,128)(2,1)}, u32[]{:S(2)}) copy-start(bf16[8,8,8,8]{0,3,2,1:T(8,128)(2,1)} %get-tuple-element.118) | copy-start | bytes 24580
  254.4 11.8 %copy-start.51 = (bf16[8,8,8,8]{0,3,2,1:T(8,128)(2,1)S(1)}, bf16[8,8,8,8]{0,3,2,1:T(8,128)(2,1)}, u32[]{:S(2)}) copy-start(bf16[8,8,8,8]{0,3,2,1:T(8,128)(2,1)} %get-tuple-element.114) | copy-start | bytes 24580
  255.4 11.8 %copy-start.50 = (bf16[8,8,8,8]{0,3,2,1:T(8,128)(2,1)S(1)}, bf16[8,8,8,8]{0,3,2,1:T(8,128)(2,1)}, u32[]{:S(2)}) copy-start(bf16[8,8,8,8]{0,3,2,1:T(8,128)(2,1)} %get-tuple-element.110) | copy-start | bytes 24580
  256.5 11.8 %copy-start.49 = (bf16[8,8,8,8]{0,3,2,1:T(8,128)(2,1)S(1)}, bf16[8,8,8,8]{0,3,2,1:T(8,128)(2,1)}, u32[]{:S(2)}) copy-start(bf16[8,8,8,8]{0,3,2,1:T(8,128)(2,1)} %get-tuple-element.106) | copy-start | bytes 24580
  257.6 11.8 %copy-start.48 = (bf16[8,8,8,8]{0,3,2,1:T(8,128)(2,1)S(1)}, bf16[8,8,8,8]{0,3,2,1:T(8,128)(2,1)}, u32[]{:S(2)}) copy-start(bf16[8,8,8,8]{0,3,2,1:T(8,128)(2,1)} %get-tuple-element.102) | copy-start | bytes 24580
  258.6 11.8 %copy-start.47 = (bf16[8,8,8,8]{0,3,2,1:T(8,128)(2,1)S(1)}, bf16[8,8,8,8]{0,3,2,1:T(8,128)(2,1)}, u32[]{:S(2)}) copy-start(bf16[8,8,8,8]{0,3,2,1:T(8,128)(2,1)} %get-tuple-element.98) | copy-start | bytes 24580
  259.7 11.8 %copy-start.46 = (bf16[8,8,8,8]{0,3,2,1:T(8,128)(2,1)S(1)}, bf16[8,8,8,8]{0,3,2,1:T(8,128)(2,1)}, u32[]{:S(2)}) copy-start(bf16[8,8,8,8]{0,3,2,1:T(8,128)(2,1)} %get-tuple-element.94) | copy-start | bytes 24580
  261.1 11.5 %copy-start.41 = (bf16[8,8,8,8]{0,3,2,1:T(8,128)(2,1)S(1)}, bf16[8,8,8,8]{0,3,2,1:T(8,128)(2,1)}, u32[]{:S(2)}) copy-start(bf16[8,8,8,8]{0,3,2,1:T(8,128)(2,1)} %get-tuple-element.90) | copy-start | bytes 24580
  262.2 11.5 %copy-start.37 = (bf16[8,8,8,8]{0,3,2,1:T(8,128)(2,1)S(1)}, bf16[8,8,8,8]{0,3,2,1:T(8,128)(2,1)}, u32[]{:S(2)}) copy-start(bf16[8,8,8,8]{0,3,2,1:T(8,128)(2,1)} %get-tuple-element.86) | copy-start | bytes 24580
  263.3 11.5 %copy-start.33 = (bf16[8,8,8,8]{0,3,2,1:T(8,128)(2,1)S(1)}, bf16[8,8,8,8]{0,3,2,1:T(8,128)(2,1)}, u32[]{:S(2)}) copy-start(bf16[8,8,8,8]{0,3,2,1:T(8,128)(2,1)} %get-tuple-element.82) | copy-start | bytes 24580
  264.3 11.5 %copy-start.28 = (bf16[8,8,8,8]{0,3,2,1:T(8,128)(2,1)S(1)}, bf16[8,8,8,8]{0,3,2,1:T(8,128)(2,1)}, u32[]{:S(2)}) copy-start(bf16[8,8,8,8]{0,3,2,1:T(8,128)(2,1)} %get-tuple-element.78) | copy-start | bytes 24580
  265.4 11.4 %copy-start.24 = (bf16[8,8,8,8]{0,3,2,1:T(8,128)(2,1)S(1)}, bf16[8,8,8,8]{0,3,2,1:T(8,128)(2,1)}, u32[]{:S(2)}) copy-start(bf16[8,8,8,8]{0,3,2,1:T(8,128)(2,1)} %get-tuple-element.74) | copy-start | bytes 24580
  266.5 11.5 %copy-start.20 = (bf16[8,8,8,8]{0,3,2,1:T(8,128)(2,1)S(1)}, bf16[8,8,8,8]{0,3,2,1:T(8,128)(2,1)}, u32[]{:S(2)}) copy-start(bf16[8,8,8,8]{0,3,2,1:T(8,128)(2,1)} %get-tuple-element.70) | copy-start | bytes 24580
  267.6 11.5 %copy-start.15 = (bf16[8,8,8,8]{0,3,2,1:T(8,128)(2,1)S(1)}, bf16[8,8,8,8]{0,3,2,1:T(8,128)(2,1)}, u32[]{:S(2)}) copy-start(bf16[8,8,8,8]{0,3,2,1:T(8,128)(2,1)} %get-tuple-element.66) | copy-start | bytes 24580
  268.6 11.5 %copy-start.11 = (bf16[8,8,8,8]{0,3,2,1:T(8,128)(2,1)S(1)}, bf16[8,8,8,8]{0,3,2,1:T(8,128)(2,1)}, u32[]{:S(2)}) copy-start(bf16[8,8,8,8]{0,3,2,1:T(8,128)(2,1)} %get-tuple-element.62) | copy-start | bytes 24580
  270.8 12.4 %copy-start.45 = (bf16[8,8,8,8]{0,3,2,1:T(8,128)(2,1)S(1)}, bf16[8,8,8,8]{0,3,2,1:T(8,128)(2,1)}, u32[]{:S(2)}) copy-start(bf16[8,8,8,8]{0,3,2,1:T(8,128)(2,1)} %get-tuple-element.60) | copy-start | bytes 24580
  271.8 11.8 %copy-start.44 = (bf16[8,8,8,8]{0,3,2,1:T(8,128)(2,1)S(1)}, bf16[8,8,8,8]{0,3,2,1:T(8,128)(2,1)}, u32[]{:S(2)}) copy-start(bf16[8,8,8,8]{0,3,2,1:T(8,128)(2,1)} %get-tuple-element.61) | copy-start | bytes 24580
  (95 other events, 592.5 us)
Sparse Core Ops, SparseCore 0:
  330.2 455.2 all-reduce.3
where the time goes:
time: 803 us; the launch traced here: 797 us
  waiting for transfers between devices  455 us (57%)
  local copies, waits for them, and re-layouts  152 us (19%)
  blocking collectives  114 us (14%)
  other arithmetic  39.4 us (5%)
  between operations  17.8 us (2%)
  matrix products  9.76 us (1%)
  starting transfers between devices  9.69 us (1%)
    psum x1, waiting for transfers between devices, shards(): summed = lax.psum(packed, ('stream', 'cross'))  455 us
    another operation x126, local copies, waits for them, and re-layouts, stencil(): return jnp.stack(columns)  77.5 us
    all_gather x1, blocking collectives, shards(): lax.all_gather(target[KEEP:], 'cross', axis=0, tiled=True)  60.5 us
    all_gather x1, blocking collectives, shards(): lax.all_gather(flat_rows[KEEP:], 'cross', axis=0, tiled=True)  53 us
    slice x125, local copies, waits for them, and re-layouts, stencil(): padded[:, along_x:along_x + block_edge, along_y:along_y + block_edge, alo...  38.1 us
    concatenate x31, other arithmetic, shards(): work_padded = jnp.concatenate([padded[:KEEP], got_blocks], axis=0)  34.8 us
  transfers between devices with their start and end apart: 5, of which 1 were waited for; matrix products, arithmetic and copies ran while one was open for 1% of the time, Pallas kernels for 0%

commit v1 on v0

--- a/solution.py
+++ b/solution.py
@@ -115,7 +115,10 @@
     flat_rows = jnp.pad(flat_rows, ((0, 0), (0, PADROW - padded_edge**3)))
     pieces = (
         lax.all_gather(flat_rows[KEEP:], "cross", axis=0, tiled=True),
-        lax.all_gather(target[KEEP:], "cross", axis=0, tiled=True),
+        jnp.concatenate(
+            lax.all_to_all(jnp.stack([target[KEEP:]] * lax.axis_size("cross")), "cross", 0, 0),
+            axis=0,
+        ),
     )
     selector = (chosen[:, None] == jnp.arange(pieces[0].shape[0])[None, :]).astype(jnp.bfloat16)
     got_blocks = jnp.dot(selector, pieces[0], preferred_element_type=jnp.float32)

time: 803 us -> 779 us (0.970)
  blocking collectives: 114 us -> 57.4 us
  starting transfers between devices: 9.69 us -> 29.5 us
    all_gather x1 -> x0, blocking collectives: 60.5 us -> none  [shards(): lax.all_gather(target[KEEP:], 'cross', axis=0, tiled=True)]
    all_to_all x0 -> x1, starting transfers between devices: none -> 18.7 us  [shards(): lax.all_to_all(jnp.stack([target[KEEP:]] * lax.axis_size('cross')), 'cros...]
  transfers between devices with their start and end apart: 5 -> 6, of which waited for: 1 -> 2; matrix products, arithmetic and copies ran while one was open for 1% -> 25% of each run, Pallas kernels for 0% -> 0%
where the time goes in v1:
time: 779 us; the launch traced here: 773 us
  waiting for transfers between devices  456 us (59%)
  local copies, waits for them, and re-layouts  160 us (21%)
  blocking collectives  57.4 us (7%)
  other arithmetic  40.1 us (5%)
  starting transfers between devices  29.5 us (4%)
  between operations  17.9 us (2%)
  matrix products  11.7 us (2%)
    psum x1, waiting for transfers between devices, shards(): summed = lax.psum(packed, ('stream', 'cross'))  455 us
    another operation x126, local copies, waits for them, and re-layouts, stencil(): return jnp.stack(columns)  82.3 us
    all_gather x1, blocking collectives, shards(): lax.all_gather(flat_rows[KEEP:], 'cross', axis=0, tiled=True)  57.4 us
    slice x125, local copies, waits for them, and re-layouts, stencil(): padded[:, along_x:along_x + block_edge, along_y:along_y + block_edge, alo...  39.3 us
    concatenate x31, other arithmetic, shards(): work_padded = jnp.concatenate([padded[:KEEP], got_blocks], axis=0)  35.6 us
    all_to_all x1, starting transfers between devices, shards(): lax.all_to_all(jnp.stack([target[KEEP:]] * lax.axis_size('cross')), 'cros...  18.7 us
  transfers between devices with their start and end apart: 6, of which 2 were waited for; matrix products, arithmetic and copies ran while one was open for 25% of the time, Pallas kernels for 0%

profile of v1, /device:TPU:1, one launch (start us, length us, event | category | flops | bytes accessed | tf_op | source)
XLA Modules:
  0.0 772.6 jit_solution(3373470099756317012)
XLA Ops:
  7.2 4.0 collective-permute-start
  11.2 1.3 collective-permute-start.1
  12.5 1.4 fusion.44
  14.6 18.7 %all-to-all-start = ((bf16[32,6,512]{2,1,0:T(8,128)(2,1)}), bf16[32,6,512]{2,1,0:T(8,128)(2,1)S(1)}, u32[]{:S(2)}, u32[]{:S(2)}) async-start(bf16[32,6,512]{2,1,0:T(8,128)(2,1)} %stack.35), calls=%async_computation | async-start | bytes 524288 | tf_op jit(solution)/shard_map/all_to_all | solution.py:119
  36.4 3.5 collective-permute-start.2
  39.9 1.9 collective-permute-start.3
  43.2 1.2 convert_element_type.65
  45.8 2.0 gather_fusion
  48.2 7.5 reshape.52
  55.7 12.7 %copy.151 = bf16[12,3,8,3,8,3,8]{0,6,5,4,3,2,1:T(8,128)(2,1)} copy(bf16[12,3,8,3,8,3,8]{6,4,2,5,3,1,0:T(8,128)(2,1)} %bitcast.316) | data formatting | bytes 663552 | tf_op jit(solution)/shard_map/transpose | solution.py:23
  68.4 1.4 slice.565
  69.8 1.4 slice.564
  71.7 57.4 %all-gather = bf16[32,6,1792]{2,1,0:T(8,128)(2,1)S(1)} all-gather(bf16[1,6,1792]{2,1,0:T(8,128)(2,1)S(1)} %fusion.18), channel_id=1, replica_groups=mesh['stream'=16,'cross'=32] {'cross'}, dimensions={0}, use_global_device_ids=true | all-gather | bytes 709632 | tf_op jit(solution)/shard_map/all_gather | solution.py:117
  129.7 1.0 copy.153
  131.3 1.2 slice_maximum_fusion.12
  132.4 1.1 slice_maximum_fusion.13
  133.6 1.3 slice_maximum_fusion.14
  134.9 1.3 slice_maximum_fusion.15
  136.2 1.3 slice_maximum_fusion.16
  137.4 1.1 slice_maximum_fusion.17
  138.6 1.1 slice_maximum_fusion.18
  139.7 1.3 slice_maximum_fusion.19
  141.0 1.3 slice_maximum_fusion.20
  142.2 1.2 slice_maximum_fusion.21
  143.5 1.2 slice_maximum_fusion.22
  144.7 1.1 slice_maximum_fusion.23
  145.9 1.3 slice_maximum_fusion.24
  147.1 1.3 slice_maximum_fusion.25
  148.4 1.2 slice_maximum_fusion.26
  149.7 1.2 slice_maximum_fusion.27
  150.9 1.2 slice_maximum_fusion.28
  152.0 1.2 slice_maximum_fusion.29
  153.2 1.2 slice_maximum_fusion.11
  154.4 1.3 slice_maximum_fusion.10
  155.7 1.3 slice_maximum_fusion.9
  157.0 1.1 slice_maximum_fusion.8
  158.1 1.4 slice_maximum_fusion.7
  159.5 1.2 slice_maximum_fusion.6
  160.7 1.2 slice_maximum_fusion.5
  161.9 1.2 slice_maximum_fusion.4
  163.1 1.2 slice_maximum_fusion.3
  164.3 1.1 slice_maximum_fusion.2
  168.1 0.8 stack_reshape.378
  172.4 0.8 stack_reshape.417
  176.4 1.2 copy.200
  201.2 0.8 stack_reshape.443
  226.9 1.2 stack_reshape.467
  240.0 0.8 stack_reshape.479
  244.3 0.8 stack_reshape.483
  248.3 1.2 copy.191
  250.2 1.2 copy.192
  252.2 1.2 copy.193
  280.8 10.4 %stack.34 = bf16[125,4096]{1,0:T(8,128)(2,1)S(1)} concatenate(bf16[1,4096]{1,0:T(2,128)(2,1)S(1)} %stack_reshape.375, bf16[1,4096]{1,0:T(2,128)(2,1)S(1)} %stack_reshape.376, bf16[1,4096]{1,0:T(2,128)(2,1)S(1)} %stack_reshape.377, bf16[1,4096]{1,0:T(2,128)(2,1)S(1)} %copy-done.110, bf16[1,4096]{1,0:T(2,128)(2,1)S(1)} %stack_reshape.379, bf16[1,4096]{1,0:T(2,128)(2,1)S(1)} %stack_reshape.380, ...), dimensions={0} | concatenate | bytes 2048000 | tf_op jit(solution)/shard_map/stack | solution.py:43
  292.1 1.0 copy-done.1
  294.7 1.1 convolution_convert_fusion
  295.9 2.8 fusion.3
  298.7 2.7 fusion.6
  301.4 1.8 convolution_bitcast_fusion.1
  303.3 1.1 convolution_bitcast_fusion
  304.6 0.8 pad_maximum_fusion.1
  306.1 455.2 %all-reduce.4.cloned.1.call-done = f32[384,128]{1,0:T(8,128)} async-done(((f32[384,128]{1,0:T(8,128)}), f32[384,128]{1,0:T(8,128)}) %all-reduce.4.cloned.1.call-update) | async-done | bytes 196624 | tf_op jit(solution)/shard_map/psum | solution.py:154
  761.3 1.6 slice.816
  762.9 1.5 slice.815
  764.4 1.2 slice_bitcast_fusion
  (600 shorter events, 114.3 us)
Async XLA Ops:
  7.2 284.0 %copy-start = (bf16[125,128]{1,0:T(8,128)(2,1)S(1)}, bf16[125,128]{1,0:T(8,128)(2,1)}, u32[]{:S(2)}) copy-start(bf16[125,128]{1,0:T(8,128)(2,1)} %param.13) | copy-start | bytes 96004
  7.2 28.5 %collective-permute-start = (bf16[12,512]{1,0:T(8,128)(2,1)}, bf16[12,512]{1,0:T(8,128)(2,1)S(1)}, u32[]{:S(2)}, u32[]{:S(2)}) collective-permute-start(bf16[12,512]{1,0:T(8,128)(2,1)} %param.8), channel_id=1, source_target_pairs={{0,32},{32,64},{64,96},{96,128},{128,160},{160,192},{192,224},{224... | collective-permute-start | bytes 36872 | tf_op jit(solution)/shard_map/ppermute | solution.py:16
  11.2 24.4 %collective-permute-start.1 = (bf16[12,512]{1,0:T(8,128)(2,1)}, bf16[12,512]{1,0:T(8,128)(2,1)S(1)}, u32[]{:S(2)}, u32[]{:S(2)}) collective-permute-start(bf16[12,512]{1,0:T(8,128)(2,1)} %param.8), channel_id=1, source_target_pairs={{32,0},{64,32},{96,64},{128,96},{160,128},{192,160},{224,192},{256... | collective-permute-start | bytes 36872 | tf_op jit(solution)/shard_map/ppermute | solution.py:16
  14.6 279.3 %all-to-all-start = ((bf16[32,6,512]{2,1,0:T(8,128)(2,1)}), bf16[32,6,512]{2,1,0:T(8,128)(2,1)S(1)}, u32[]{:S(2)}, u32[]{:S(2)}) async-start(bf16[32,6,512]{2,1,0:T(8,128)(2,1)} %stack.35), calls=%async_computation | async-start | bytes 524288 | tf_op jit(solution)/shard_map/all_to_all | solution.py:119
  33.3 728.0 %all-reduce.4.cloned.1.call-start = ((), (), s32[]{:S(2)}) async-start(), calls=%async_computation.1 | async-start | bytes 393216 | tf_op jit(solution)/shard_map/psum | solution.py:154
  36.4 8.7 %collective-permute-start.2 = (bf16[3,12,512]{2,1,0:T(8,128)(2,1)S(1)}, bf16[3,12,512]{2,1,0:T(8,128)(2,1)S(1)}, u32[]{:S(2)}, u32[]{:S(2)}) collective-permute-start(bf16[3,12,512]{2,1,0:T(8,128)(2,1)S(1)} %get-tuple-element.137), channel_id=1, source_target_pairs={{0,1},{1,2},{2,3},{3,4},{4,5},{5,6},{6,7},{7,8},{8,9},{9,10},{10,1... | collective-permute-start | bytes 110600 | tf_op jit(solution)/shard_map/ppermute | solution.py:16
  39.9 5.7 collective-permute-start.3
  71.3 58.1 %copy-start.153 = (s32[1,2]{1,0:T(1,128)S(1)}, s32[1,2]{1,0:T(1,128)}, u32[]{:S(2)}) copy-start(s32[1,2]{1,0:T(1,128)} %param.12) | copy-start | bytes 28
  167.7 11.7 %copy-start.101 = (bf16[8,8,8,8]{0,3,2,1:T(8,128)(2,1)S(1)}, bf16[8,8,8,8]{0,3,2,1:T(8,128)(2,1)}, u32[]{:S(2)}) copy-start(bf16[8,8,8,8]{0,3,2,1:T(8,128)(2,1)} %get-tuple-element.73) | copy-start | bytes 24580
  168.1 12.3 %copy-start.100 = (bf16[8,8,8,8]{0,3,2,1:T(8,128)(2,1)S(1)}, bf16[8,8,8,8]{0,3,2,1:T(8,128)(2,1)}, u32[]{:S(2)}) copy-start(bf16[8,8,8,8]{0,3,2,1:T(8,128)(2,1)} %get-tuple-element.75) | copy-start | bytes 24580
  169.2 12.3 %copy-start.99 = (bf16[8,8,8,8]{0,3,2,1:T(8,128)(2,1)S(1)}, bf16[8,8,8,8]{0,3,2,1:T(8,128)(2,1)}, u32[]{:S(2)}) copy-start(bf16[8,8,8,8]{0,3,2,1:T(8,128)(2,1)} %get-tuple-element.76) | copy-start | bytes 24580
  170.3 12.3 %copy-start.98 = (bf16[8,8,8,8]{0,3,2,1:T(8,128)(2,1)S(1)}, bf16[8,8,8,8]{0,3,2,1:T(8,128)(2,1)}, u32[]{:S(2)}) copy-start(bf16[8,8,8,8]{0,3,2,1:T(8,128)(2,1)} %get-tuple-element.77) | copy-start | bytes 24580
  171.3 12.3 %copy-start.97 = (bf16[8,8,8,8]{0,3,2,1:T(8,128)(2,1)S(1)}, bf16[8,8,8,8]{0,3,2,1:T(8,128)(2,1)}, u32[]{:S(2)}) copy-start(bf16[8,8,8,8]{0,3,2,1:T(8,128)(2,1)} %get-tuple-element.79) | copy-start | bytes 24580
  172.4 12.3 %copy-start.96 = (bf16[8,8,8,8]{0,3,2,1:T(8,128)(2,1)S(1)}, bf16[8,8,8,8]{0,3,2,1:T(8,128)(2,1)}, u32[]{:S(2)}) copy-start(bf16[8,8,8,8]{0,3,2,1:T(8,128)(2,1)} %get-tuple-element.80) | copy-start | bytes 24580
  173.5 12.3 %copy-start.95 = (bf16[8,8,8,8]{0,3,2,1:T(8,128)(2,1)S(1)}, bf16[8,8,8,8]{0,3,2,1:T(8,128)(2,1)}, u32[]{:S(2)}) copy-start(bf16[8,8,8,8]{0,3,2,1:T(8,128)(2,1)} %get-tuple-element.81) | copy-start | bytes 24580
  174.6 12.3 %copy-start.94 = (bf16[8,8,8,8]{0,3,2,1:T(8,128)(2,1)S(1)}, bf16[8,8,8,8]{0,3,2,1:T(8,128)(2,1)}, u32[]{:S(2)}) copy-start(bf16[8,8,8,8]{0,3,2,1:T(8,128)(2,1)} %get-tuple-element.83) | copy-start | bytes 24580
  175.6 12.3 %copy-start.93 = (bf16[8,8,8,8]{0,3,2,1:T(8,128)(2,1)S(1)}, bf16[8,8,8,8]{0,3,2,1:T(8,128)(2,1)}, u32[]{:S(2)}) copy-start(bf16[8,8,8,8]{0,3,2,1:T(8,128)(2,1)} %get-tuple-element.84) | copy-start | bytes 24580
  180.8 11.6 %copy-start.89 = (bf16[8,8,8,8]{0,3,2,1:T(8,128)(2,1)S(1)}, bf16[8,8,8,8]{0,3,2,1:T(8,128)(2,1)}, u32[]{:S(2)}) copy-start(bf16[8,8,8,8]{0,3,2,1:T(8,128)(2,1)} %get-tuple-element.89) | copy-start | bytes 24580
  181.8 11.6 %copy-start.88 = (bf16[8,8,8,8]{0,3,2,1:T(8,128)(2,1)S(1)}, bf16[8,8,8,8]{0,3,2,1:T(8,128)(2,1)}, u32[]{:S(2)}) copy-start(bf16[8,8,8,8]{0,3,2,1:T(8,128)(2,1)} %get-tuple-element.91) | copy-start | bytes 24580
  182.9 11.6 %copy-start.87 = (bf16[8,8,8,8]{0,3,2,1:T(8,128)(2,1)S(1)}, bf16[8,8,8,8]{0,3,2,1:T(8,128)(2,1)}, u32[]{:S(2)}) copy-start(bf16[8,8,8,8]{0,3,2,1:T(8,128)(2,1)} %get-tuple-element.92) | copy-start | bytes 24580
  184.0 11.6 %copy-start.86 = (bf16[8,8,8,8]{0,3,2,1:T(8,128)(2,1)S(1)}, bf16[8,8,8,8]{0,3,2,1:T(8,128)(2,1)}, u32[]{:S(2)}) copy-start(bf16[8,8,8,8]{0,3,2,1:T(8,128)(2,1)} %get-tuple-element.93) | copy-start | bytes 24580
  185.0 11.6 %copy-start.85 = (bf16[8,8,8,8]{0,3,2,1:T(8,128)(2,1)S(1)}, bf16[8,8,8,8]{0,3,2,1:T(8,128)(2,1)}, u32[]{:S(2)}) copy-start(bf16[8,8,8,8]{0,3,2,1:T(8,128)(2,1)} %get-tuple-element.95) | copy-start | bytes 24580
  186.1 11.6 %copy-start.84 = (bf16[8,8,8,8]{0,3,2,1:T(8,128)(2,1)S(1)}, bf16[8,8,8,8]{0,3,2,1:T(8,128)(2,1)}, u32[]{:S(2)}) copy-start(bf16[8,8,8,8]{0,3,2,1:T(8,128)(2,1)} %get-tuple-element.96) | copy-start | bytes 24580
  187.2 11.6 %copy-start.83 = (bf16[8,8,8,8]{0,3,2,1:T(8,128)(2,1)S(1)}, bf16[8,8,8,8]{0,3,2,1:T(8,128)(2,1)}, u32[]{:S(2)}) copy-start(bf16[8,8,8,8]{0,3,2,1:T(8,128)(2,1)} %get-tuple-element.97) | copy-start | bytes 24580
  188.2 11.6 %copy-start.82 = (bf16[8,8,8,8]{0,3,2,1:T(8,128)(2,1)S(1)}, bf16[8,8,8,8]{0,3,2,1:T(8,128)(2,1)}, u32[]{:S(2)}) copy-start(bf16[8,8,8,8]{0,3,2,1:T(8,128)(2,1)} %get-tuple-element.99) | copy-start | bytes 24580
  189.3 11.6 %copy-start.81 = (bf16[8,8,8,8]{0,3,2,1:T(8,128)(2,1)S(1)}, bf16[8,8,8,8]{0,3,2,1:T(8,128)(2,1)}, u32[]{:S(2)}) copy-start(bf16[8,8,8,8]{0,3,2,1:T(8,128)(2,1)} %get-tuple-element.100) | copy-start | bytes 24580
  190.4 11.6 %copy-start.80 = (bf16[8,8,8,8]{0,3,2,1:T(8,128)(2,1)S(1)}, bf16[8,8,8,8]{0,3,2,1:T(8,128)(2,1)}, u32[]{:S(2)}) copy-start(bf16[8,8,8,8]{0,3,2,1:T(8,128)(2,1)} %get-tuple-element.101) | copy-start | bytes 24580
  191.6 11.5 %copy-start.79 = (bf16[8,8,8,8]{0,3,2,1:T(8,128)(2,1)S(1)}, bf16[8,8,8,8]{0,3,2,1:T(8,128)(2,1)}, u32[]{:S(2)}) copy-start(bf16[8,8,8,8]{0,3,2,1:T(8,128)(2,1)} %get-tuple-element.103) | copy-start | bytes 24580
  192.7 11.5 %copy-start.78 = (bf16[8,8,8,8]{0,3,2,1:T(8,128)(2,1)S(1)}, bf16[8,8,8,8]{0,3,2,1:T(8,128)(2,1)}, u32[]{:S(2)}) copy-start(bf16[8,8,8,8]{0,3,2,1:T(8,128)(2,1)} %get-tuple-element.104) | copy-start | bytes 24580
  193.8 11.5 %copy-start.77 = (bf16[8,8,8,8]{0,3,2,1:T(8,128)(2,1)S(1)}, bf16[8,8,8,8]{0,3,2,1:T(8,128)(2,1)}, u32[]{:S(2)}) copy-start(bf16[8,8,8,8]{0,3,2,1:T(8,128)(2,1)} %get-tuple-element.105) | copy-start | bytes 24580
  194.8 11.5 %copy-start.76 = (bf16[8,8,8,8]{0,3,2,1:T(8,128)(2,1)S(1)}, bf16[8,8,8,8]{0,3,2,1:T(8,128)(2,1)}, u32[]{:S(2)}) copy-start(bf16[8,8,8,8]{0,3,2,1:T(8,128)(2,1)} %get-tuple-element.107) | copy-start | bytes 24580
  195.9 11.5 %copy-start.75 = (bf16[8,8,8,8]{0,3,2,1:T(8,128)(2,1)S(1)}, bf16[8,8,8,8]{0,3,2,1:T(8,128)(2,1)}, u32[]{:S(2)}) copy-start(bf16[8,8,8,8]{0,3,2,1:T(8,128)(2,1)} %get-tuple-element.108) | copy-start | bytes 24580
  197.0 11.5 %copy-start.74 = (bf16[8,8,8,8]{0,3,2,1:T(8,128)(2,1)S(1)}, bf16[8,8,8,8]{0,3,2,1:T(8,128)(2,1)}, u32[]{:S(2)}) copy-start(bf16[8,8,8,8]{0,3,2,1:T(8,128)(2,1)} %get-tuple-element.109) | copy-start | bytes 24580
  198.0 11.5 %copy-start.73 = (bf16[8,8,8,8]{0,3,2,1:T(8,128)(2,1)S(1)}, bf16[8,8,8,8]{0,3,2,1:T(8,128)(2,1)}, u32[]{:S(2)}) copy-start(bf16[8,8,8,8]{0,3,2,1:T(8,128)(2,1)} %get-tuple-element.111) | copy-start | bytes 24580
  199.1 11.4 %copy-start.72 = (bf16[8,8,8,8]{0,3,2,1:T(8,128)(2,1)S(1)}, bf16[8,8,8,8]{0,3,2,1:T(8,128)(2,1)}, u32[]{:S(2)}) copy-start(bf16[8,8,8,8]{0,3,2,1:T(8,128)(2,1)} %get-tuple-element.112) | copy-start | bytes 24580
  200.2 11.5 %copy-start.71 = (bf16[8,8,8,8]{0,3,2,1:T(8,128)(2,1)S(1)}, bf16[8,8,8,8]{0,3,2,1:T(8,128)(2,1)}, u32[]{:S(2)}) copy-start(bf16[8,8,8,8]{0,3,2,1:T(8,128)(2,1)} %get-tuple-element.113) | copy-start | bytes 24580
  201.2 11.5 %copy-start.70 = (bf16[8,8,8,8]{0,3,2,1:T(8,128)(2,1)S(1)}, bf16[8,8,8,8]{0,3,2,1:T(8,128)(2,1)}, u32[]{:S(2)}) copy-start(bf16[8,8,8,8]{0,3,2,1:T(8,128)(2,1)} %get-tuple-element.115) | copy-start | bytes 24580
  202.3 11.4 %copy-start.69 = (bf16[8,8,8,8]{0,3,2,1:T(8,128)(2,1)S(1)}, bf16[8,8,8,8]{0,3,2,1:T(8,128)(2,1)}, u32[]{:S(2)}) copy-start(bf16[8,8,8,8]{0,3,2,1:T(8,128)(2,1)} %get-tuple-element.116) | copy-start | bytes 24580
  203.4 11.4 %copy-start.68 = (bf16[8,8,8,8]{0,3,2,1:T(8,128)(2,1)S(1)}, bf16[8,8,8,8]{0,3,2,1:T(8,128)(2,1)}, u32[]{:S(2)}) copy-start(bf16[8,8,8,8]{0,3,2,1:T(8,128)(2,1)} %get-tuple-element.117) | copy-start | bytes 24580
  204.4 11.5 %copy-start.67 = (bf16[8,8,8,8]{0,3,2,1:T(8,128)(2,1)S(1)}, bf16[8,8,8,8]{0,3,2,1:T(8,128)(2,1)}, u32[]{:S(2)}) copy-start(bf16[8,8,8,8]{0,3,2,1:T(8,128)(2,1)} %get-tuple-element.119) | copy-start | bytes 24580
  205.5 11.5 %copy-start.66 = (bf16[8,8,8,8]{0,3,2,1:T(8,128)(2,1)S(1)}, bf16[8,8,8,8]{0,3,2,1:T(8,128)(2,1)}, u32[]{:S(2)}) copy-start(bf16[8,8,8,8]{0,3,2,1:T(8,128)(2,1)} %get-tuple-element.120) | copy-start | bytes 24580
  206.6 11.5 %copy-start.65 = (bf16[8,8,8,8]{0,3,2,1:T(8,128)(2,1)S(1)}, bf16[8,8,8,8]{0,3,2,1:T(8,128)(2,1)}, u32[]{:S(2)}) copy-start(bf16[8,8,8,8]{0,3,2,1:T(8,128)(2,1)} %get-tuple-element.121) | copy-start | bytes 24580
  207.6 11.5 %copy-start.64 = (bf16[8,8,8,8]{0,3,2,1:T(8,128)(2,1)S(1)}, bf16[8,8,8,8]{0,3,2,1:T(8,128)(2,1)}, u32[]{:S(2)}) copy-start(bf16[8,8,8,8]{0,3,2,1:T(8,128)(2,1)} %get-tuple-element.123) | copy-start | bytes 24580
  208.7 11.5 %copy-start.63 = (bf16[8,8,8,8]{0,3,2,1:T(8,128)(2,1)S(1)}, bf16[8,8,8,8]{0,3,2,1:T(8,128)(2,1)}, u32[]{:S(2)}) copy-start(bf16[8,8,8,8]{0,3,2,1:T(8,128)(2,1)} %get-tuple-element.124) | copy-start | bytes 24580
  210.8 11.4 %copy-start.61 = (bf16[8,8,8,8]{0,3,2,1:T(8,128)(2,1)S(1)}, bf16[8,8,8,8]{0,3,2,1:T(8,128)(2,1)}, u32[]{:S(2)}) copy-start(bf16[8,8,8,8]{0,3,2,1:T(8,128)(2,1)} %get-tuple-element.127) | copy-start | bytes 24580
  213.0 11.5 %copy-start.59 = (bf16[8,8,8,8]{0,3,2,1:T(8,128)(2,1)S(1)}, bf16[8,8,8,8]{0,3,2,1:T(8,128)(2,1)}, u32[]{:S(2)}) copy-start(bf16[8,8,8,8]{0,3,2,1:T(8,128)(2,1)} %get-tuple-element.129) | copy-start | bytes 24580
  214.0 11.4 %copy-start.58 = (bf16[8,8,8,8]{0,3,2,1:T(8,128)(2,1)S(1)}, bf16[8,8,8,8]{0,3,2,1:T(8,128)(2,1)}, u32[]{:S(2)}) copy-start(bf16[8,8,8,8]{0,3,2,1:T(8,128)(2,1)} %get-tuple-element.131) | copy-start | bytes 24580
  215.1 11.5 %copy-start.57 = (bf16[8,8,8,8]{0,3,2,1:T(8,128)(2,1)S(1)}, bf16[8,8,8,8]{0,3,2,1:T(8,128)(2,1)}, u32[]{:S(2)}) copy-start(bf16[8,8,8,8]{0,3,2,1:T(8,128)(2,1)} %get-tuple-element.132) | copy-start | bytes 24580
  216.2 11.8 %copy-start.56 = (bf16[8,8,8,8]{0,3,2,1:T(8,128)(2,1)S(1)}, bf16[8,8,8,8]{0,3,2,1:T(8,128)(2,1)}, u32[]{:S(2)}) copy-start(bf16[8,8,8,8]{0,3,2,1:T(8,128)(2,1)} %get-tuple-element.133) | copy-start | bytes 24580
  217.2 11.8 %copy-start.55 = (bf16[8,8,8,8]{0,3,2,1:T(8,128)(2,1)S(1)}, bf16[8,8,8,8]{0,3,2,1:T(8,128)(2,1)}, u32[]{:S(2)}) copy-start(bf16[8,8,8,8]{0,3,2,1:T(8,128)(2,1)} %get-tuple-element.130) | copy-start | bytes 24580
  218.3 11.8 %copy-start.54 = (bf16[8,8,8,8]{0,3,2,1:T(8,128)(2,1)S(1)}, bf16[8,8,8,8]{0,3,2,1:T(8,128)(2,1)}, u32[]{:S(2)}) copy-start(bf16[8,8,8,8]{0,3,2,1:T(8,128)(2,1)} %get-tuple-element.126) | copy-start | bytes 24580
  219.4 11.8 %copy-start.53 = (bf16[8,8,8,8]{0,3,2,1:T(8,128)(2,1)S(1)}, bf16[8,8,8,8]{0,3,2,1:T(8,128)(2,1)}, u32[]{:S(2)}) copy-start(bf16[8,8,8,8]{0,3,2,1:T(8,128)(2,1)} %get-tuple-element.122) | copy-start | bytes 24580
  220.4 11.8 %copy-start.52 = (bf16[8,8,8,8]{0,3,2,1:T(8,128)(2,1)S(1)}, bf16[8,8,8,8]{0,3,2,1:T(8,128)(2,1)}, u32[]{:S(2)}) copy-start(bf16[8,8,8,8]{0,3,2,1:T(8,128)(2,1)} %get-tuple-element.118) | copy-start | bytes 24580
  221.5 11.8 %copy-start.51 = (bf16[8,8,8,8]{0,3,2,1:T(8,128)(2,1)S(1)}, bf16[8,8,8,8]{0,3,2,1:T(8,128)(2,1)}, u32[]{:S(2)}) copy-start(bf16[8,8,8,8]{0,3,2,1:T(8,128)(2,1)} %get-tuple-element.114) | copy-start | bytes 24580
  222.6 11.8 %copy-start.50 = (bf16[8,8,8,8]{0,3,2,1:T(8,128)(2,1)S(1)}, bf16[8,8,8,8]{0,3,2,1:T(8,128)(2,1)}, u32[]{:S(2)}) copy-start(bf16[8,8,8,8]{0,3,2,1:T(8,128)(2,1)} %get-tuple-element.110) | copy-start | bytes 24580
  223.6 11.8 %copy-start.49 = (bf16[8,8,8,8]{0,3,2,1:T(8,128)(2,1)S(1)}, bf16[8,8,8,8]{0,3,2,1:T(8,128)(2,1)}, u32[]{:S(2)}) copy-start(bf16[8,8,8,8]{0,3,2,1:T(8,128)(2,1)} %get-tuple-element.106) | copy-start | bytes 24580
  224.7 11.8 %copy-start.48 = (bf16[8,8,8,8]{0,3,2,1:T(8,128)(2,1)S(1)}, bf16[8,8,8,8]{0,3,2,1:T(8,128)(2,1)}, u32[]{:S(2)}) copy-start(bf16[8,8,8,8]{0,3,2,1:T(8,128)(2,1)} %get-tuple-element.102) | copy-start | bytes 24580
  225.8 11.8 %copy-start.47 = (bf16[8,8,8,8]{0,3,2,1:T(8,128)(2,1)S(1)}, bf16[8,8,8,8]{0,3,2,1:T(8,128)(2,1)}, u32[]{:S(2)}) copy-start(bf16[8,8,8,8]{0,3,2,1:T(8,128)(2,1)} %get-tuple-element.98) | copy-start | bytes 24580
  226.9 11.8 %copy-start.46 = (bf16[8,8,8,8]{0,3,2,1:T(8,128)(2,1)S(1)}, bf16[8,8,8,8]{0,3,2,1:T(8,128)(2,1)}, u32[]{:S(2)}) copy-start(bf16[8,8,8,8]{0,3,2,1:T(8,128)(2,1)} %get-tuple-element.94) | copy-start | bytes 24580
  240.0 14.1 %copy-start.45 = (bf16[8,8,8,8]{0,3,2,1:T(8,128)(2,1)S(1)}, bf16[8,8,8,8]{0,3,2,1:T(8,128)(2,1)}, u32[]{:S(2)}) copy-start(bf16[8,8,8,8]{0,3,2,1:T(8,128)(2,1)} %get-tuple-element.58) | copy-start | bytes 24580
  241.1 13.5 %copy-start.44 = (bf16[8,8,8,8]{0,3,2,1:T(8,128)(2,1)S(1)}, bf16[8,8,8,8]{0,3,2,1:T(8,128)(2,1)}, u32[]{:S(2)}) copy-start(bf16[8,8,8,8]{0,3,2,1:T(8,128)(2,1)} %get-tuple-element.55) | copy-start | bytes 24580
  242.2 12.9 %copy-start.42 = (bf16[8,8,8,8]{0,3,2,1:T(8,128)(2,1)S(1)}, bf16[8,8,8,8]{0,3,2,1:T(8,128)(2,1)}, u32[]{:S(2)}) copy-start(bf16[8,8,8,8]{0,3,2,1:T(8,128)(2,1)} %get-tuple-element.56) | copy-start | bytes 24580
  243.2 12.3 %copy-start.41 = (bf16[8,8,8,8]{0,3,2,1:T(8,128)(2,1)S(1)}, bf16[8,8,8,8]{0,3,2,1:T(8,128)(2,1)}, u32[]{:S(2)}) copy-start(bf16[8,8,8,8]{0,3,2,1:T(8,128)(2,1)} %get-tuple-element.57) | copy-start | bytes 24580
  244.3 11.7 %copy-start.40 = (bf16[8,8,8,8]{0,3,2,1:T(8,128)(2,1)S(1)}, bf16[8,8,8,8]{0,3,2,1:T(8,128)(2,1)}, u32[]{:S(2)}) copy-start(bf16[8,8,8,8]{0,3,2,1:T(8,128)(2,1)} %get-tuple-element.54) | copy-start | bytes 24580
  (98 other events, 642.5 us)
Sparse Core Ops, SparseCore 0:
  305.6 455.6 all-reduce.3
